TPU v7x, 32 devices: a whole 2x2x4 slice. The times are simulated.
32 devices in a mesh: row: 8 (over z, x), slab: 4 (over y, core).
Axes of the slice: x: 2, y: 2, z: 4, core: 2. Of those that a mesh axis runs over, the one named last changes fastest.
Arguments:
- base_features: bfloat16 [64, 2048], P(None, ('row', 'slab')), may hold values from -0.8984375 to 0.8984375
- station_ids: int32 [2048], P(('row', 'slab')), may hold values from 0 to 511
- epoch_ids: int32 [2048], P(('row', 'slab')), may hold values from 0 to 511
- station_table: bfloat16 [64, 512], replicated, may hold values from -0.8984375 to 0.8984375
- epoch_table: bfloat16 [64, 512], replicated, may hold values from -0.8984375 to 0.8984375
- noise_var: float32 [2048], P(('row', 'slab')), may hold values from 0.05 to 1
- right_side: float32 [32, 2048], P(None, ('row', 'slab')), may hold values from -6 to 6
Outputs:
- solution: float32 [32, 2048], P(None, ('row', 'slab'))
- residual: float32 [32, 2048], P(None, ('row', 'slab'))
All inputs are finite; a program needn't handle non-finite values.
Results may differ from a plain program's by a relative error of at most 0.012.
The roundings to bfloat16 on the way count: a program that leaves them out, or rounds other values in their place, can miss the bound.
Values may be sent and summed in bfloat16 or wider, within the bound.
A program may use at most 64 MiB of HBM per device.

v0:
```python
import jax
import jax.numpy as jnp
from jax import lax
from jax.sharding import PartitionSpec as P

ITERS = 2


def lookup(table, indices):
    positions = lax.broadcasted_iota(jnp.int32, (table.shape[1], indices.shape[0]), 0)
    one_hot = (positions == indices[None, :]).astype(jnp.bfloat16)
    return jnp.dot(table, one_hot, preferred_element_type=jnp.float32)


def column_norms(piece):
    wide_piece = piece.astype(jnp.float32)
    return jnp.sum(wide_piece * wide_piece, axis=0)


def tile_term(col_feat, col_dir, rows_feat, rows_norm):
    cross_term = lax.dot_general(
        col_feat, rows_feat, (((0,), (0,)), ((), ())), preferred_element_type=jnp.float32
    )
    col_norm = column_norms(col_feat)
    distance = jnp.maximum(col_norm[:, None] + rows_norm[None, :] - 2.0 * cross_term, 0.0)
    kernel_tile = jnp.exp(-0.5 * distance).astype(jnp.bfloat16)
    return jnp.dot(col_dir, kernel_tile, preferred_element_type=jnp.float32)


def global_dot(left, right):
    return lax.psum(jnp.sum(left * right, axis=1), ("row", "slab"))


def per_device(
    base_features, station_ids, epoch_ids, station_table, epoch_table, noise_var, right_side
):
    own_feat = (
        base_features.astype(jnp.float32)
        + lookup(station_table, station_ids)
        + lookup(epoch_table, epoch_ids)
    ).astype(jnp.bfloat16)
    rows_feat = lax.all_gather(own_feat, "slab", axis=1, tiled=True)
    rows_norm = column_norms(rows_feat)
    solution = jnp.zeros_like(right_side)
    residual = right_side
    direction = right_side
    res_norm = global_dot(residual, residual)
    for iteration in range(ITERS):
        rounded = direction.astype(jnp.bfloat16)
        partial_value = tile_term(
            lax.all_gather(own_feat, "row", axis=1, tiled=True),
            lax.all_gather(rounded, "row", axis=1, tiled=True),
            rows_feat,
            rows_norm,
        )
        product = lax.psum_scatter(partial_value, "slab", scatter_dimension=1, tiled=True)
        image = product + noise_var[None, :] * direction
        curvature = global_dot(direction, image)
        step_size = res_norm / curvature
        solution = solution + step_size[:, None] * direction
        residual = residual - step_size[:, None] * image
        if iteration + 1 < ITERS:
            new_norm = global_dot(residual, residual)
            direction = residual + (new_norm / res_norm)[:, None] * direction
            res_norm = new_norm
    return (solution, residual)


def solution(mesh):
    in_specs = (
        P(None, ("row", "slab")),
        P(("row", "slab")),
        P(("row", "slab")),
        P(),
        P(),
        P(("row", "slab")),
        P(None, ("row", "slab")),
    )
    out_specs = (P(None, ("row", "slab")), P(None, ("row", "slab")))
    return jax.shard_map(
        per_device, mesh=mesh, in_specs=in_specs, out_specs=out_specs, check_vma=False
    )
```

profile of v0, /device:TPU:0, one launch (start us, length us, event | category | flops | bytes accessed | tf_op | source)
XLA Modules:
  0.0 280.7 jit_solution(9992201375895917600)
XLA Ops:
  7.2 0.8 copy.13
  8.1 0.2 fusion.6
  8.3 0.6 copy-done.3
  8.9 0.2 fusion.7
  9.1 32.3 %all_gather.13 = bf16[64,512]{0,1:T(8,128)(2,1)S(1)} all-gather(bf16[64,64]{0,1:T(8,128)(2,1)S(1)} %fusion.7), channel_id=1, replica_groups=mesh['row'=8,'slab'=4] {'row'}, dimensions={1}, use_global_device_ids=true | all-gather | bytes 73728 | tf_op jit(solution)/shard_map/all_gather | solution.py:51
  41.4 5.2 %all_gather.14 = bf16[64,256]{0,1:T(8,128)(2,1)S(1)} all-gather(bf16[64,64]{0,1:T(8,128)(2,1)S(1)} %fusion.7), channel_id=1, replica_groups=mesh['row'=8,'slab'=4] {'slab'}, dimensions={1}, use_global_device_ids=true | all-gather | bytes 40960 | tf_op jit(solution)/shard_map/all_gather | solution.py:42
  46.7 0.1 multiply_reduce_fusion
  46.9 0.6 copy-done.1
  47.5 30.5 %all-gather = bf16[8,64,32]{1,2,0:T(8,128)(2,1)S(1)} all-gather(bf16[1,64,32]{1,2,0:T(8,128)(2,1)S(1)} %convert_bitcast_fusion.1), channel_id=1, replica_groups=mesh['row'=8,'slab'=4] {'row'}, dimensions={0}, use_global_device_ids=true | all-gather | bytes 36864 | tf_op jit(solution)/shard_map/all_gather | solution.py:52
  78.2 0.3 fusion.4
  78.5 0.1 convolution_bitcast_fusion.1
  78.6 0.7 copy.16
  79.4 20.6 %reduce-scatter.7.cloned.1.call-done = f32[64,32]{1,0:T(8,128)} async-done(((f32[256,32]{1,0:T(8,128)}), f32[64,32]{1,0:T(8,128)}) %reduce-scatter.7.cloned.1.call-update) | async-done | bytes 8208
  100.1 0.8 copy.17
  101.0 39.4 %all-reduce = (f32[32]{0:T(128)S(1)}, f32[32]{0:T(128)S(1)}) all-reduce(f32[32]{0:T(128)S(1)} %get-tuple-element.3, f32[32]{0:T(128)S(1)} %get-tuple-element.2), channel_id=1, replica_groups=mesh['row'=8,'slab'=4] {'row','slab'}, use_global_device_ids=true, to_apply=%region_1.0 | all-reduce | flops 64 | bytes 512 | tf_op jit(solution)/shard_map/psum | solution.py:31
  140.4 0.2 multiply_reduce_fusion.3
  140.6 41.0 %psum.30 = f32[32]{0:T(128)S(1)} all-reduce(f32[32]{0:T(128)S(1)} %multiply_reduce_fusion.3), channel_id=1, replica_groups=mesh['row'=8,'slab'=4] {'row','slab'}, use_global_device_ids=true, to_apply=%region_8.0 | all-reduce | flops 32 | bytes 256 | tf_op jit(solution)/shard_map/psum | solution.py:31
  181.7 30.5 %all-gather.1 = bf16[8,64,32]{1,2,0:T(8,128)(2,1)S(1)} all-gather(bf16[1,64,32]{1,2,0:T(8,128)(2,1)S(1)} %convert_bitcast_fusion), channel_id=1, replica_groups=mesh['row'=8,'slab'=4] {'row'}, dimensions={0}, use_global_device_ids=true | all-gather | bytes 36864 | tf_op jit(solution)/shard_map/all_gather | solution.py:52
  212.3 0.9 convolution_bitcast_fusion
  213.3 19.5 %reduce-scatter.9.cloned.1.call-done = f32[64,32]{1,0:T(8,128)} async-done(((f32[256,32]{1,0:T(8,128)}), f32[64,32]{1,0:T(8,128)}) %reduce-scatter.9.cloned.1.call-update) | async-done | bytes 8208
  232.8 0.8 copy.19
  233.6 0.2 multiply_reduce_fusion.2
  233.8 39.4 %psum.31 = f32[32]{0:T(128)S(1)} all-reduce(f32[32]{0:T(128)S(1)} %multiply_reduce_fusion.2), channel_id=1, replica_groups=mesh['row'=8,'slab'=4] {'row','slab'}, use_global_device_ids=true, to_apply=%region_11.0 | all-reduce | flops 32 | bytes 256 | tf_op jit(solution)/shard_map/psum | solution.py:31
  273.1 0.7 multiply_subtract_fusion
  (25 shorter events, 0.8 us)
Async XLA Ops:
  7.2 0.9 copy-start
  7.2 0.9 copy-start.4
  7.2 92.9 %reduce-scatter.7.cloned.1.call-start = ((), (), s32[]{:S(2)}) async-start(), calls=%async_computation.2 | async-start | bytes 163840
  8.1 0.8 copy-start.3
  8.1 0.8 copy-start.5
  46.8 0.7 copy-start.1
  79.4 153.4 %reduce-scatter.9.cloned.1.call-start = ((), (), s32[]{:S(2)}) async-start(), calls=%async_computation.3 | async-start | bytes 163840
  100.1 0.8 copy-start.2
Sparse Core Ops, SparseCore 0:
  79.5 20.5 reduce-scatter.6
  213.4 19.3 reduce-scatter.8
where the time goes:
time: 282 us; the launch traced here: 281 us
  blocking collectives  218 us (77%)
  waiting for transfers between devices  40.1 us (14%)
  between operations  14.1 us (5%)
  local copies, waits for them, and re-layouts  4.73 us (2%)
    psum x3, blocking collectives, global_dot(): return lax.psum(jnp.sum(left * right, axis=1), ('row', 'slab'))  120 us
    all_gather x2, blocking collectives, per_device(): lax.all_gather(rounded, 'row', axis=1, tiled=True)  61 us
    unnamed x4, waiting for transfers between devices  40.1 us
    all_gather x1, blocking collectives, per_device(): lax.all_gather(own_feat, 'row', axis=1, tiled=True)  32.3 us
  transfers between devices with their start and end apart: 2, of which 2 were waited for; matrix products, arithmetic and copies ran while one was open for 0% of the time, Pallas kernels for 0%

commit v1 on v0

--- a/solution.py
+++ b/solution.py
@@ -1,6 +1,10 @@
+import functools
+
 import jax
 import jax.numpy as jnp
 from jax import lax
+from jax.experimental import pallas as pl
+from jax.experimental.pallas import tpu as pltpu
 from jax.sharding import PartitionSpec as P
 
 ITERS = 2
@@ -66,6 +70,269 @@
     return (solution, residual)
 
 
+MESH = pl.DeviceIdType.MESH
+NT = (((1,), (1,)), ((), ()))
+HALF = 64
+
+
+def dot_nt(left, right, precision=None):
+    return lax.dot_general(left, right, NT, precision=precision, preferred_element_type=jnp.float32)
+
+
+def lane_mask(rows):
+    return lax.broadcasted_iota(jnp.int32, (rows, 128), 1) < HALF
+
+
+def swap(value):
+    return pltpu.roll(value, HALF, 1)
+
+
+def fold(wide, odd):
+    half = wide.shape[0] // 2
+    top, bottom = wide[:half], wide[half:]
+    if odd:
+        return jnp.where(lane_mask(half), swap(top), bottom)
+    return jnp.where(lane_mask(half), top, swap(bottom))
+
+
+def unfold_pair(first, second):
+    mask = lane_mask(first.shape[0])
+    top = jnp.where(mask, first, swap(second))
+    bottom = jnp.where(mask, swap(first), second)
+    return jnp.concatenate([top, bottom], axis=0)
+
+
+def unfold_all(blocks):
+    pairs = [unfold_pair(blocks[k], blocks[k + 1]) for k in range(0, len(blocks), 2)]
+    return jnp.concatenate(pairs, axis=1)
+
+
+def split_rows(folded):
+    mask = lane_mask(folded.shape[0])
+    zero = jnp.zeros_like(folded)
+    return jnp.concatenate([jnp.where(mask, folded, zero), jnp.where(mask, zero, folded)], axis=0)
+
+
+def solve_kernel(
+    n_row, n_slab,
+    base_hbm, sid_hbm, eid_hbm, station_hbm, epoch_hbm, noise_hbm, right_hbm,
+    sol_out, res_out,
+    base_v, sid_v, eid_v, station_v, epoch_v, noise_v, right_v,
+    col_v, row_v, kernel_v, part1_v, sum1_v, qcol_v, qrow_v, part2_v, sum2_v, mom_v, mom_in,
+    load_sem, s_g1, r_g1, s_g1r, r_g1r, s_rs1, r_rs1, s_g2, r_g2, s_g2r, r_g2r, s_rs2, r_rs2, s_ar, r_ar,
+):
+    row, slab = lax.axis_index("row"), lax.axis_index("slab")
+    feat, samples = base_hbm.shape
+    vecs = right_hbm.shape[0]
+    n_dev = n_row * n_slab
+
+    def row_peer(k):
+        return (lax.rem(row + k, n_row), slab)
+
+    def slab_peer(k):
+        return (row, lax.rem(slab + k, n_slab))
+
+    def remote(src, dst, send, recv, peer):
+        copy = pltpu.make_async_remote_copy(
+            src_ref=src, dst_ref=dst, send_sem=send, recv_sem=recv, device_id=peer, device_id_type=MESH
+        )
+        copy.start()
+        return copy
+
+    barrier = pltpu.get_barrier_semaphore()
+    for k in range(1, n_row):
+        pl.semaphore_signal(barrier, inc=1, device_id=row_peer(k), device_id_type=MESH)
+    for k in range(1, n_slab):
+        pl.semaphore_signal(barrier, inc=1, device_id=slab_peer(k), device_id_type=MESH)
+
+    loads = []
+    for k, (src, dst) in enumerate((
+        (sid_hbm, sid_v), (eid_hbm, eid_v), (station_hbm, station_v), (epoch_hbm, epoch_v),
+        (base_hbm, base_v), (right_hbm, right_v), (noise_hbm, noise_v),
+    )):
+        copy = pltpu.make_async_copy(src, dst, load_sem.at[k])
+        copy.start()
+        loads.append(copy)
+    for copy in loads:
+        copy.wait()
+
+    def gather(table, ids):
+        positions = lax.broadcasted_iota(jnp.int32, (table.shape[1], samples), 0)
+        one_hot = jnp.where(positions == ids, 1.0, 0.0).astype(jnp.bfloat16)
+        return jnp.dot(table, one_hot, preferred_element_type=jnp.float32)
+
+    right = right_v[...]
+    own = (
+        base_v[...].astype(jnp.float32)
+        + gather(station_v[...], sid_v[...])
+        + gather(epoch_v[...], eid_v[...])
+    ).astype(jnp.bfloat16).astype(jnp.float32)
+    norm = -0.5 * jnp.sum(own * own, axis=0, keepdims=True)
+    high = norm.astype(jnp.bfloat16).astype(jnp.float32)
+    middle = (norm - high).astype(jnp.bfloat16).astype(jnp.float32)
+    low = norm - high - middle
+    at = lax.broadcasted_iota(jnp.int32, (8, samples), 0)
+    one, nil = jnp.ones((8, samples), jnp.float32), jnp.zeros((8, samples), jnp.float32)
+    col_norm = jnp.where(at == 0, high, jnp.where(at == 1, middle, jnp.where(at == 2, low, jnp.where(at < 6, one, nil))))
+    row_norm = jnp.where(at < 3, one, jnp.where(at == 3, high, jnp.where(at == 4, middle, jnp.where(at == 5, low, nil))))
+    rest = jnp.zeros((128 - feat - vecs - 8, samples), jnp.float32)
+    stacked = jnp.concatenate(
+        [own, right, col_norm, rest, own, jnp.zeros((vecs, samples), jnp.float32), row_norm, rest], axis=0
+    ).astype(jnp.bfloat16)
+    eye_r = lax.broadcasted_iota(jnp.int32, (samples, samples), 0)
+    eye_c = lax.broadcasted_iota(jnp.int32, (samples, samples), 1)
+    eye = jnp.where(eye_r == eye_c, 1.0, 0.0).astype(jnp.bfloat16)
+    packs = dot_nt(eye, stacked).astype(jnp.bfloat16)
+    col_v[0] = packs[:, :128]
+    row_v[0] = packs[:, 128:]
+
+    pl.semaphore_wait(barrier, n_row + n_slab - 2)
+    g1 = [remote(col_v.at[0], col_v.at[k], s_g1.at[k], r_g1.at[k], row_peer(k)) for k in range(1, n_row)]
+    g1 += [remote(row_v.at[0], row_v.at[k], s_g1r.at[k], r_g1r.at[k], slab_peer(k)) for k in range(1, n_slab)]
+
+    half = vecs // 2
+    right_f = jnp.concatenate([right[:half], right[half:]], axis=1)
+    noise_f = jnp.concatenate([noise_v[...], noise_v[...]], axis=1)
+    pick_r = lax.broadcasted_iota(jnp.int32, (vecs, 128), 0)
+    pick_c = lax.broadcasted_iota(jnp.int32, (vecs, 128), 1)
+    pick = jnp.where(pick_c == pick_r + feat, 1.0, 0.0).astype(jnp.bfloat16)
+
+    for copy in g1:
+        copy.wait_recv()
+
+    cols = col_v[...].reshape(n_row * samples, 128)
+    rows = row_v[...].reshape(n_slab * samples, 128)
+    logits = dot_nt(cols, rows)
+    directions = dot_nt(pick, cols).astype(jnp.bfloat16)
+    kernel_v[...] = jnp.exp(jnp.minimum(logits, 0.0)).astype(jnp.bfloat16)
+    tile = kernel_v[...]
+    part = jnp.dot(directions, tile, preferred_element_type=jnp.float32)
+
+    def reduce_start(part, out_v, in_v, send, recv):
+        copies = []
+        for k in range(n_slab - 1, -1, -1):
+            start = 128 * (k // 2)
+            out_v[k] = fold(part[:, start:start + 128], k % 2)
+            if k:
+                copies.append(remote(out_v.at[k], in_v.at[k], send.at[k], recv.at[k], slab_peer(n_slab - k)))
+        return copies
+
+    def reduce_end(copies, out_v, in_v):
+        for copy in copies:
+            copy.wait_recv()
+        total = out_v[0]
+        for k in range(1, n_slab):
+            total = total + in_v[k]
+        return total
+
+    rs1 = reduce_start(part, part1_v, sum1_v, s_rs1, r_rs1)
+    image = reduce_end(rs1, part1_v, sum1_v) + noise_f * right_f
+
+    rounded = image.astype(jnp.bfloat16)
+    qcol_v[0] = rounded
+    g2 = [remote(qcol_v.at[0], qcol_v.at[k], s_g2.at[k], r_g2.at[k], row_peer(k)) for k in range(1, n_row)]
+    g2 += [remote(qcol_v.at[0], qrow_v.at[k], s_g2r.at[k], r_g2r.at[k], slab_peer(k)) for k in range(1, n_slab)]
+    qrow_v[0] = rounded
+
+    early = jnp.concatenate(
+        [split_rows(right_f * right_f), split_rows(right_f * image), split_rows(image * image),
+         split_rows(noise_f * image * image)], axis=0
+    )
+    moments = dot_nt(jnp.ones((8, 128), jnp.float32), early, lax.Precision.HIGHEST)
+
+    for copy in g2:
+        copy.wait_recv()
+    images = unfold_all([qcol_v[k].astype(jnp.float32) for k in range(n_row)]).astype(jnp.bfloat16)
+    part = jnp.dot(images, tile, preferred_element_type=jnp.float32)
+    rs2 = reduce_start(part, part2_v, sum2_v, s_rs2, r_rs2)
+    own_rows = unfold_all([qrow_v[k].astype(jnp.float32) for k in range(n_slab)])
+    late = jnp.concatenate([jnp.zeros((3 * vecs, part.shape[1]), jnp.float32), own_rows * part], axis=0)
+    moments = moments + dot_nt(jnp.ones((8, part.shape[1]), jnp.float32), late, lax.Precision.HIGHEST)
+    mom_v[...] = moments[:1]
+
+    me = row * n_slab + slab
+    ar = []
+    for k in range(1, n_dev):
+        other = lax.rem(me + k, n_dev)
+        peer = (other // n_slab, lax.rem(other, n_slab))
+        ar.append(remote(mom_v, mom_in.at[k], s_ar.at[k], r_ar.at[k], peer))
+    second = reduce_end(rs2, part2_v, sum2_v) + noise_f * image
+    mask = lane_mask(half)
+    image_n = jnp.concatenate([image, swap(image)], axis=0)[:, :samples]
+    second_n = jnp.concatenate([second, swap(second)], axis=0)[:, :samples]
+
+    for copy in ar:
+        copy.wait_recv()
+    total = mom_v[...]
+    for k in range(1, n_dev):
+        total = total + mom_in[k]
+    total = jnp.broadcast_to(total, (8, 128))
+    bb = total
+    bq, qq, qs = (pltpu.roll(total, 128 - vecs * k, 1) for k in (1, 2, 3))
+    alpha = bb / bq
+    fresh = bb - 2.0 * alpha * bq + alpha * alpha * qq
+    grow = 1.0 + fresh / bb
+    curvature = grow * grow * bq - 2.0 * alpha * grow * qq + alpha * alpha * qs
+    step = fresh / curvature
+    first_c = alpha + step * grow
+    second_c = step * alpha
+
+    def column(coefficients):
+        spread = jnp.where(pick_r == pick_c, coefficients[:1], 0.0)
+        return jnp.sum(spread, axis=1, keepdims=True)
+
+    first_c, second_c = column(first_c), column(second_c)
+    sol_out[...] = first_c * right - second_c * image_n
+    res_out[...] = right - first_c * image_n + second_c * second_n
+
+    for copy in g1 + rs1 + g2 + rs2 + ar:
+        copy.wait_send()
+
+
+def per_device_kernel(
+    n_row, n_slab, base_features, station_ids, epoch_ids, station_table, epoch_table, noise_var, right_side
+):
+    feat, samples = base_features.shape
+    vecs = right_side.shape[0]
+    n_dev = n_row * n_slab
+    bf16, f32 = jnp.bfloat16, jnp.float32
+    dma = pltpu.SemaphoreType.DMA
+    half = vecs // 2
+    operands = (
+        base_features, station_ids.reshape(1, samples), epoch_ids.reshape(1, samples),
+        station_table, epoch_table, noise_var.reshape(1, samples), right_side,
+    )
+    shape = jax.ShapeDtypeStruct((vecs, samples), f32)
+    return pl.pallas_call(
+        functools.partial(solve_kernel, n_row, n_slab),
+        out_shape=(shape, shape),
+        in_specs=[pl.BlockSpec(memory_space=pl.ANY)] * 7,
+        out_specs=(pl.BlockSpec(memory_space=pltpu.VMEM),) * 2,
+        scratch_shapes=[pltpu.VMEM(x.shape, x.dtype) for x in operands] + [
+            pltpu.VMEM((n_row, samples, 128), bf16),
+            pltpu.VMEM((n_slab, samples, 128), bf16),
+            pltpu.VMEM((n_row * samples, n_slab * samples), bf16),
+            pltpu.VMEM((n_slab, half, 128), f32),
+            pltpu.VMEM((n_slab, half, 128), f32),
+            pltpu.VMEM((n_row, half, 128), bf16),
+            pltpu.VMEM((n_slab, half, 128), bf16),
+            pltpu.VMEM((n_slab, half, 128), f32),
+            pltpu.VMEM((n_slab, half, 128), f32),
+            pltpu.VMEM((1, 128), f32),
+            pltpu.VMEM((n_dev, 1, 128), f32),
+            dma((7,)),
+            dma((n_row,)), dma((n_row,)), dma((n_slab,)), dma((n_slab,)),
+            dma((n_slab,)), dma((n_slab,)),
+            dma((n_row,)), dma((n_row,)), dma((n_slab,)), dma((n_slab,)),
+            dma((n_slab,)), dma((n_slab,)),
+            dma((n_dev,)), dma((n_dev,)),
+        ],
+        compiler_params=pltpu.CompilerParams(
+            collective_id=0, has_side_effects=True, vmem_limit_bytes=16 * 1024 * 1024
+        ),
+    )(*operands)
+
+
 def solution(mesh):
     in_specs = (
         P(None, ("row", "slab")),
@@ -77,6 +344,10 @@
         P(None, ("row", "slab")),
     )
     out_specs = (P(None, ("row", "slab")), P(None, ("row", "slab")))
+    n_row, n_slab = mesh.shape["row"], mesh.shape["slab"]
+    body = per_device
+    if n_row * n_slab <= 64:
+        body = functools.partial(per_device_kernel, n_row, n_slab)
     return jax.shard_map(
-        per_device, mesh=mesh, in_specs=in_specs, out_specs=out_specs, check_vma=False
-    )
+        body, mesh=mesh, in_specs=in_specs, out_specs=out_specs, check_vma=False
+    )

time: 282 us -> 30.1 us (0.11)
  blocking collectives: 218 us -> 0 us
  waiting for transfers between devices: 40.1 us -> 0 us
  Pallas kernels: 0 us -> 24.1 us
  between operations: 14.1 us -> 0.67 us
    psum x3 -> x0, blocking collectives: 120 us -> none  [global_dot(): return lax.psum(jnp.sum(left * right, axis=1), ('row', 'slab'))]
    all_gather x4 -> x0, blocking collectives: 98.5 us -> none  [the longest x2 61 us: per_device(): lax.all_gather(rounded, 'row', axis=1, tiled=True)]
    unnamed x4 -> x0, waiting for transfers between devices: 40.1 us -> none
    pallas_call x0 -> x1, Pallas kernels: none -> 24.1 us  [per_device_kernel(): pl.pallas_call(functools.partial(solve_kernel, n_row, n_slab), out_shape=...]
  transfers between devices with their start and end apart: 2 -> 0, of which waited for: 2 -> 0; matrix products, arithmetic and copies ran while one was open for 0% -> 0% of each run, Pallas kernels for 0% -> 0%
where the time goes in v1:
time: 30.1 us; the launch traced here: 29.8 us
  Pallas kernels  24.1 us (80%)
  local copies, waits for them, and re-layouts  4.99 us (17%)
  between operations  0.67 us (2%)
    pallas_call x1, Pallas kernels, per_device_kernel(): pl.pallas_call(functools.partial(solve_kernel, n_row, n_slab), out_shape=...  24.1 us
    unnamed x16, local copies, waits for them, and re-layouts  4.99 us

profile of v1, /device:TPU:0, one launch (start us, length us, event | category | flops | bytes accessed | tf_op | source)
XLA Modules:
  0.0 29.8 jit_solution(17322798180798758621)
XLA Ops:
  0.6 0.0 copy-start.4
  0.6 0.0 copy-start.5
  0.7 0.0 copy-start.6
  0.7 0.6 %copy-done.4 = s32[64]{0:T(128)S(1)} copy-done((s32[64]{0:T(128)S(1)}, s32[64]{0:T(128)}, u32[]{:S(2)}) %copy-start.4) | copy-done | bytes 280
  1.3 0.0 copy-done.5
  1.3 0.0 copy-done.6
  1.3 0.0 copy-start
  1.3 0.8 %copy-done = bf16[64,512]{1,0:T(8,128)(2,1)S(1)} copy-done((bf16[64,512]{1,0:T(8,128)(2,1)S(1)}, bf16[64,512]{1,0:T(8,128)(2,1)}, u32[]{:S(2)}) %copy-start) | copy-done | bytes 65560
  2.2 0.0 copy-start.1
  2.2 0.8 %copy-done.1 = bf16[64,512]{1,0:T(8,128)(2,1)S(1)} copy-done((bf16[64,512]{1,0:T(8,128)(2,1)S(1)}, bf16[64,512]{1,0:T(8,128)(2,1)}, u32[]{:S(2)}) %copy-start.1) | copy-done | bytes 65560
  3.0 0.0 copy-start.2
  3.0 0.7 %copy-done.2 = bf16[64,64]{1,0:T(8,128)(2,1)S(1)} copy-done((bf16[64,64]{1,0:T(8,128)(2,1)S(1)}, bf16[64,64]{1,0:T(8,128)(2,1)}, u32[]{:S(2)}) %copy-start.2) | copy-done | bytes 8216
  3.7 0.0 copy-start.3
  3.7 0.7 %copy-done.3 = f32[32,64]{1,0:T(8,128)S(1)} copy-done((f32[32,64]{1,0:T(8,128)S(1)}, f32[32,64]{1,0:T(8,128)}, u32[]{:S(2)}) %copy-start.3) | copy-done | bytes 8216
  4.4 24.1 %shard_map.86 = (f32[32,64]{1,0:T(8,128)S(1)}, f32[32,64]{1,0:T(8,128)S(1)}) custom-call(bf16[64,64]{1,0:T(8,128)(2,1)S(1)} %copy-done.2, s32[1,64]{1,0:T(1,128)S(1)} %bitcast.3, s32[1,64]{1,0:T(1,128)S(1)} %bitcast.4, bf16[64,512]{1,0:T(8,128)(2,1)S(1)} %copy-done, bf16[64,512]{1,0:T(8,128)(2,1)S(1)} %copy-done.1, f32[1,64]{1,0:T(1,128)S(1)} %bitcast.5, ...), custom_call_target="tpu_custom_call" | custom-call | tf_op jit(solution)/shard_map/pallas_call | solution.py:306
  28.6 0.6 %copy.11 = f32[32,64]{1,0:T(8,128)} copy(f32[32,64]{1,0:T(8,128)S(1)} %get-tuple-element.4) | data formatting | bytes 16384
  29.2 0.6 %copy.12 = f32[32,64]{1,0:T(8,128)} copy(f32[32,64]{1,0:T(8,128)S(1)} %get-tuple-element.5) | data formatting | bytes 16384
Async XLA Ops:
  0.6 0.7 %copy-start.4 = (s32[64]{0:T(128)S(1)}, s32[64]{0:T(128)}, u32[]{:S(2)}) copy-start(s32[64]{0:T(128)} %param.8) | copy-start | bytes 772
  0.6 0.7 %copy-start.5 = (s32[64]{0:T(128)S(1)}, s32[64]{0:T(128)}, u32[]{:S(2)}) copy-start(s32[64]{0:T(128)} %param.9) | copy-start | bytes 772
  0.7 0.7 %copy-start.6 = (f32[64]{0:T(128)S(1)}, f32[64]{0:T(128)}, u32[]{:S(2)}) copy-start(f32[64]{0:T(128)} %param.12) | copy-start | bytes 772
  1.3 0.8 %copy-start = (bf16[64,512]{1,0:T(8,128)(2,1)S(1)}, bf16[64,512]{1,0:T(8,128)(2,1)}, u32[]{:S(2)}) copy-start(bf16[64,512]{1,0:T(8,128)(2,1)} %station_hbm.1) | copy-start | bytes 196612
  2.2 0.8 %copy-start.1 = (bf16[64,512]{1,0:T(8,128)(2,1)S(1)}, bf16[64,512]{1,0:T(8,128)(2,1)}, u32[]{:S(2)}) copy-start(bf16[64,512]{1,0:T(8,128)(2,1)} %epoch_hbm.1) | copy-start | bytes 196612
  3.0 0.7 %copy-start.2 = (bf16[64,64]{1,0:T(8,128)(2,1)S(1)}, bf16[64,64]{1,0:T(8,128)(2,1)}, u32[]{:S(2)}) copy-start(bf16[64,64]{1,0:T(8,128)(2,1)} %base_hbm.1) | copy-start | bytes 24580
  3.7 0.7 %copy-start.3 = (f32[32,64]{1,0:T(8,128)S(1)}, f32[32,64]{1,0:T(8,128)}, u32[]{:S(2)}) copy-start(f32[32,64]{1,0:T(8,128)} %right_hbm.1) | copy-start | bytes 24580

commit v2 on v1

--- a/solution.py
+++ b/solution.py
@@ -116,7 +116,7 @@
 def solve_kernel(
     n_row, n_slab,
     base_hbm, sid_hbm, eid_hbm, station_hbm, epoch_hbm, noise_hbm, right_hbm,
-    sol_out, res_out,
+    both_out,
     base_v, sid_v, eid_v, station_v, epoch_v, noise_v, right_v,
     col_v, row_v, kernel_v, part1_v, sum1_v, qcol_v, qrow_v, part2_v, sum2_v, mom_v, mom_in,
     load_sem, s_g1, r_g1, s_g1r, r_g1r, s_rs1, r_rs1, s_g2, r_g2, s_g2r, r_g2r, s_rs2, r_rs2, s_ar, r_ar,
@@ -247,7 +247,10 @@
     rs2 = reduce_start(part, part2_v, sum2_v, s_rs2, r_rs2)
     own_rows = unfold_all([qrow_v[k].astype(jnp.float32) for k in range(n_slab)])
     late = jnp.concatenate([jnp.zeros((3 * vecs, part.shape[1]), jnp.float32), own_rows * part], axis=0)
-    moments = moments + dot_nt(jnp.ones((8, part.shape[1]), jnp.float32), late, lax.Precision.HIGHEST)
+    ones = jnp.ones((8, part.shape[1]), jnp.bfloat16)
+    late_high = late.astype(jnp.bfloat16)
+    late_low = (late - late_high.astype(jnp.float32)).astype(jnp.bfloat16)
+    moments = moments + (dot_nt(ones, late_high) + dot_nt(ones, late_low))
     mom_v[...] = moments[:1]
 
     me = row * n_slab + slab
@@ -282,8 +285,8 @@
         return jnp.sum(spread, axis=1, keepdims=True)
 
     first_c, second_c = column(first_c), column(second_c)
-    sol_out[...] = first_c * right - second_c * image_n
-    res_out[...] = right - first_c * image_n + second_c * second_n
+    both_out[0] = first_c * right - second_c * image_n
+    both_out[1] = right - first_c * image_n + second_c * second_n
 
     for copy in g1 + rs1 + g2 + rs2 + ar:
         copy.wait_send()
@@ -302,12 +305,12 @@
         base_features, station_ids.reshape(1, samples), epoch_ids.reshape(1, samples),
         station_table, epoch_table, noise_var.reshape(1, samples), right_side,
     )
-    shape = jax.ShapeDtypeStruct((vecs, samples), f32)
-    return pl.pallas_call(
+    shape = jax.ShapeDtypeStruct((2, vecs, samples), f32)
+    both = pl.pallas_call(
         functools.partial(solve_kernel, n_row, n_slab),
-        out_shape=(shape, shape),
+        out_shape=shape,
         in_specs=[pl.BlockSpec(memory_space=pl.ANY)] * 7,
-        out_specs=(pl.BlockSpec(memory_space=pltpu.VMEM),) * 2,
+        out_specs=pl.BlockSpec(memory_space=pltpu.VMEM),
         scratch_shapes=[pltpu.VMEM(x.shape, x.dtype) for x in operands] + [
             pltpu.VMEM((n_row, samples, 128), bf16),
             pltpu.VMEM((n_slab, samples, 128), bf16),
@@ -328,9 +331,10 @@
             dma((n_dev,)), dma((n_dev,)),
         ],
         compiler_params=pltpu.CompilerParams(
-            collective_id=0, has_side_effects=True, vmem_limit_bytes=16 * 1024 * 1024
+            collective_id=0, has_side_effects=True, vmem_limit_bytes=60 * 1024 * 1024
         ),
     )(*operands)
+    return both[0], both[1]
 
 
 def solution(mesh):

time: 30.1 us -> 26.7 us (0.89)
  local copies, waits for them, and re-layouts: 4.99 us -> 1.35 us
  Pallas kernels: 24.1 us -> 24.5 us
    unnamed x16 -> x0, local copies, waits for them, and re-layouts: 4.99 us -> none
    squeeze x0 -> x1, local copies, waits for them, and re-layouts: none -> 1.35 us  [per_device_kernel(): return (both[0], both[1])]
    pallas_call x1, Pallas kernels: 24.1 us -> 24.5 us  [per_device_kernel(): pl.pallas_call(functools.partial(solve_kernel, n_row, n_slab), out_shape=...]
where the time goes in v2:
time: 26.7 us; the launch traced here: 26.4 us
  Pallas kernels  24.5 us (92%)
  local copies, waits for them, and re-layouts  1.35 us (5%)
  between operations  0.64 us (2%)
    pallas_call x1, Pallas kernels, per_device_kernel(): pl.pallas_call(functools.partial(solve_kernel, n_row, n_slab), out_shape=...  24.5 us
    squeeze x1, local copies, waits for them, and re-layouts, per_device_kernel(): return (both[0], both[1])  1.35 us

profile of v2, /device:TPU:0, one launch (start us, length us, event | category | flops | bytes accessed | tf_op | source)
XLA Modules:
  0.0 26.4 jit_solution(9129668952485446447)
XLA Ops:
  0.6 24.5 %shard_map.86 = f32[2,32,64]{2,1,0:T(8,128)} custom-call(bf16[64,64]{1,0:T(8,128)(2,1)} %base_hbm.1, s32[1,64]{1,0:T(1,128)} %bitcast.7, s32[1,64]{1,0:T(1,128)} %bitcast.8, bf16[64,512]{1,0:T(8,128)(2,1)} %station_hbm.1, bf16[64,512]{1,0:T(8,128)(2,1)} %epoch_hbm.1, f32[1,64]{1,0:T(1,128)} %bitcast.9, f32[32,64]{1,0:T(8,128)} %right_hbm.1), custom_call_target="tpu_custom_call" | custom-call | tf_op jit(solution)/shard_map/pallas_call | solution.py:309
  25.1 1.3 %slice_bitcast_fusion = (f32[32,64]{1,0:T(8,128)}, f32[32,64]{1,0:T(8,128)}) fusion(f32[2,32,64]{2,1,0:T(8,128)} %shard_map.86), kind=kLoop, calls=%fused_computation | loop fusion | bytes 32768 | tf_op jit(solution)/shard_map/squeeze | solution.py:337

commit v3 on v2

--- a/solution.py
+++ b/solution.py
@@ -118,8 +118,8 @@
     base_hbm, sid_hbm, eid_hbm, station_hbm, epoch_hbm, noise_hbm, right_hbm,
     both_out,
     base_v, sid_v, eid_v, station_v, epoch_v, noise_v, right_v,
-    col_v, row_v, kernel_v, part1_v, sum1_v, qcol_v, qrow_v, part2_v, sum2_v, mom_v, mom_in,
-    load_sem, s_g1, r_g1, s_g1r, r_g1r, s_rs1, r_rs1, s_g2, r_g2, s_g2r, r_g2r, s_rs2, r_rs2, s_ar, r_ar,
+    col_v, row_v, kernel_v, near_v, near_in, far_v, far_in, part2_v, sum2_v, mom_v, mom_in,
+    load_sem, s_g1, r_g1, s_g1r, r_g1r, s_g2, r_g2, s_g2r, r_g2r, s_rs2, r_rs2, s_ar, r_ar,
 ):
     row, slab = lax.axis_index("row"), lax.axis_index("slab")
     feat, samples = base_hbm.shape
@@ -225,14 +225,36 @@
             total = total + in_v[k]
         return total
 
-    rs1 = reduce_start(part, part1_v, sum1_v, s_rs1, r_rs1)
-    image = reduce_end(rs1, part1_v, sum1_v) + noise_f * right_f
-
-    rounded = image.astype(jnp.bfloat16)
-    qcol_v[0] = rounded
-    g2 = [remote(qcol_v.at[0], qcol_v.at[k], s_g2.at[k], r_g2.at[k], row_peer(k)) for k in range(1, n_row)]
-    g2 += [remote(qcol_v.at[0], qrow_v.at[k], s_g2r.at[k], r_g2r.at[k], slab_peer(k)) for k in range(1, n_slab)]
-    qrow_v[0] = rounded
+    for k in range(n_slab):
+        start = 128 * (k // 2)
+        piece = fold(part[:, start:start + 128], k % 2)
+        if k == 0:
+            piece = piece + noise_f * right_f
+        near_v[k] = piece
+        far_v[k] = piece.astype(jnp.bfloat16)
+    g2 = []
+    for j in range(1, n_row):
+        for k in range(n_slab):
+            peer = (lax.rem(row + j, n_row), lax.rem(slab + n_slab - k, n_slab))
+            g2.append(remote(far_v.at[k], far_in.at[j, k], s_g2.at[j, k], r_g2.at[j, k], peer))
+    near = [remote(near_v, near_in.at[k], s_g2r.at[k], r_g2r.at[k], slab_peer(k)) for k in range(1, n_slab)]
+    for copy in near:
+        copy.wait_recv()
+
+    def row_image(k):
+        total = near_v[k]
+        for m in range(1, n_slab):
+            total = total + near_in[m, (k - m) % n_slab]
+        return total
+
+    row_images = [row_image(k) for k in range(n_slab)]
+    image = row_images[0]
+
+    def col_image(j):
+        total = far_in[j, 0].astype(jnp.float32)
+        for k in range(1, n_slab):
+            total = total + far_in[j, k].astype(jnp.float32)
+        return total
 
     early = jnp.concatenate(
         [split_rows(right_f * right_f), split_rows(right_f * image), split_rows(image * image),
@@ -242,10 +264,10 @@
 
     for copy in g2:
         copy.wait_recv()
-    images = unfold_all([qcol_v[k].astype(jnp.float32) for k in range(n_row)]).astype(jnp.bfloat16)
+    images = unfold_all([image] + [col_image(j) for j in range(1, n_row)]).astype(jnp.bfloat16)
     part = jnp.dot(images, tile, preferred_element_type=jnp.float32)
     rs2 = reduce_start(part, part2_v, sum2_v, s_rs2, r_rs2)
-    own_rows = unfold_all([qrow_v[k].astype(jnp.float32) for k in range(n_slab)])
+    own_rows = unfold_all(row_images)
     late = jnp.concatenate([jnp.zeros((3 * vecs, part.shape[1]), jnp.float32), own_rows * part], axis=0)
     ones = jnp.ones((8, part.shape[1]), jnp.bfloat16)
     late_high = late.astype(jnp.bfloat16)
@@ -288,7 +310,7 @@
     both_out[0] = first_c * right - second_c * image_n
     both_out[1] = right - first_c * image_n + second_c * second_n
 
-    for copy in g1 + rs1 + g2 + rs2 + ar:
+    for copy in g1 + near + g2 + rs2 + ar:
         copy.wait_send()
 
 
@@ -316,17 +338,16 @@
             pltpu.VMEM((n_slab, samples, 128), bf16),
             pltpu.VMEM((n_row * samples, n_slab * samples), bf16),
             pltpu.VMEM((n_slab, half, 128), f32),
-            pltpu.VMEM((n_slab, half, 128), f32),
-            pltpu.VMEM((n_row, half, 128), bf16),
+            pltpu.VMEM((n_slab, n_slab, half, 128), f32),
             pltpu.VMEM((n_slab, half, 128), bf16),
+            pltpu.VMEM((n_row, n_slab, half, 128), bf16),
             pltpu.VMEM((n_slab, half, 128), f32),
             pltpu.VMEM((n_slab, half, 128), f32),
             pltpu.VMEM((1, 128), f32),
             pltpu.VMEM((n_dev, 1, 128), f32),
             dma((7,)),
             dma((n_row,)), dma((n_row,)), dma((n_slab,)), dma((n_slab,)),
-            dma((n_slab,)), dma((n_slab,)),
-            dma((n_row,)), dma((n_row,)), dma((n_slab,)), dma((n_slab,)),
+            dma((n_row, n_slab)), dma((n_row, n_slab)), dma((n_slab,)), dma((n_slab,)),
             dma((n_slab,)), dma((n_slab,)),
             dma((n_dev,)), dma((n_dev,)),
         ],

time: 26.7 us -> 25.7 us (0.963)
  Pallas kernels: 24.5 us -> 23.4 us
    pallas_call x1, Pallas kernels: 24.5 us -> 23.4 us  [per_device_kernel(): pl.pallas_call(functools.partial(solve_kernel, n_row, n_slab), out_shape=...]
where the time goes in v3:
time: 25.7 us; the launch traced here: 25.4 us
  Pallas kernels  23.4 us (91%)
  local copies, waits for them, and re-layouts  1.35 us (5%)
  between operations  0.64 us (2%)
    pallas_call x1, Pallas kernels, per_device_kernel(): pl.pallas_call(functools.partial(solve_kernel, n_row, n_slab), out_shape=...  23.4 us
    squeeze x1, local copies, waits for them, and re-layouts, per_device_kernel(): return (both[0], both[1])  1.35 us

profile of v3, /device:TPU:0, one launch (start us, length us, event | category | flops | bytes accessed | tf_op | source)
XLA Modules:
  0.0 25.4 jit_solution(15858126605971470524)
XLA Ops:
  0.6 23.4 %shard_map.86 = f32[2,32,64]{2,1,0:T(8,128)} custom-call(bf16[64,64]{1,0:T(8,128)(2,1)} %base_hbm.1, s32[1,64]{1,0:T(1,128)} %bitcast.7, s32[1,64]{1,0:T(1,128)} %bitcast.8, bf16[64,512]{1,0:T(8,128)(2,1)} %station_hbm.1, bf16[64,512]{1,0:T(8,128)(2,1)} %epoch_hbm.1, f32[1,64]{1,0:T(1,128)} %bitcast.9, f32[32,64]{1,0:T(8,128)} %right_hbm.1), custom_call_target="tpu_custom_call" | custom-call | tf_op jit(solution)/shard_map/pallas_call | solution.py:331
  24.1 1.3 %slice_bitcast_fusion = (f32[32,64]{1,0:T(8,128)}, f32[32,64]{1,0:T(8,128)}) fusion(f32[2,32,64]{2,1,0:T(8,128)} %shard_map.86), kind=kLoop, calls=%fused_computation | loop fusion | bytes 32768 | tf_op jit(solution)/shard_map/squeeze | solution.py:358

commit v4 on v3

--- a/solution.py
+++ b/solution.py
@@ -187,7 +187,7 @@
     row_v[0] = packs[:, 128:]
 
     pl.semaphore_wait(barrier, n_row + n_slab - 2)
-    g1 = [remote(col_v.at[0], col_v.at[k], s_g1.at[k], r_g1.at[k], row_peer(k)) for k in range(1, n_row)]
+    g1 = [remote(col_v.at[0], col_v.at[k], s_g1.at[k], r_g1.at[k], row_peer(k)) for k in sorted(range(1, n_row), key=lambda k: -abs(k - n_row // 2))]
     g1 += [remote(row_v.at[0], row_v.at[k], s_g1r.at[k], r_g1r.at[k], slab_peer(k)) for k in range(1, n_slab)]
 
     half = vecs // 2
@@ -233,8 +233,8 @@
         near_v[k] = piece
         far_v[k] = piece.astype(jnp.bfloat16)
     g2 = []
-    for j in range(1, n_row):
-        for k in range(n_slab):
+    for k in range(n_slab):
+        for j in sorted(range(1, n_row), key=lambda j: -abs(j - n_row // 2)):
             peer = (lax.rem(row + j, n_row), lax.rem(slab + n_slab - k, n_slab))
             g2.append(remote(far_v.at[k], far_in.at[j, k], s_g2.at[j, k], r_g2.at[j, k], peer))
     near = [remote(near_v, near_in.at[k], s_g2r.at[k], r_g2r.at[k], slab_peer(k)) for k in range(1, n_slab)]

time: 25.7 us -> 25.1 us (0.977)
  Pallas kernels: 23.4 us -> 22.8 us
    pallas_call x1, Pallas kernels: 23.4 us -> 22.8 us  [per_device_kernel(): pl.pallas_call(functools.partial(solve_kernel, n_row, n_slab), out_shape=...]
where the time goes in v4:
time: 25.1 us; the launch traced here: 24.8 us
  Pallas kernels  22.8 us (91%)
  local copies, waits for them, and re-layouts  1.35 us (5%)
  between operations  0.64 us (3%)
    pallas_call x1, Pallas kernels, per_device_kernel(): pl.pallas_call(functools.partial(solve_kernel, n_row, n_slab), out_shape=...  22.8 us
    squeeze x1, local copies, waits for them, and re-layouts, per_device_kernel(): return (both[0], both[1])  1.35 us

profile of v4, /device:TPU:0, one launch (start us, length us, event | category | flops | bytes accessed | tf_op | source)
XLA Modules:
  0.0 24.8 jit_solution(8785653677540555525)
XLA Ops:
  0.6 22.8 %shard_map.86 = f32[2,32,64]{2,1,0:T(8,128)} custom-call(bf16[64,64]{1,0:T(8,128)(2,1)} %base_hbm.1, s32[1,64]{1,0:T(1,128)} %bitcast.7, s32[1,64]{1,0:T(1,128)} %bitcast.8, bf16[64,512]{1,0:T(8,128)(2,1)} %station_hbm.1, bf16[64,512]{1,0:T(8,128)(2,1)} %epoch_hbm.1, f32[1,64]{1,0:T(1,128)} %bitcast.9, f32[32,64]{1,0:T(8,128)} %right_hbm.1), custom_call_target="tpu_custom_call" | custom-call | tf_op jit(solution)/shard_map/pallas_call | solution.py:331
  23.5 1.3 %slice_bitcast_fusion = (f32[32,64]{1,0:T(8,128)}, f32[32,64]{1,0:T(8,128)}) fusion(f32[2,32,64]{2,1,0:T(8,128)} %shard_map.86), kind=kLoop, calls=%fused_computation | loop fusion | bytes 32768 | tf_op jit(solution)/shard_map/squeeze | solution.py:358
